TPU v7x, 512 devices: a whole 4x4x16 slice. The times are simulated.
512 devices in a mesh: users: 16 (over x, z_hi, core), cand: 32 (over y, z_lo).
Axes of the slice: x: 4, y: 4, z: 16 (z_hi: 2, z_lo: 8; z = z_hi * 8 + z_lo), core: 2. Of those that a mesh axis runs over, the one named last changes fastest.
Arguments:
- cand_query: bfloat16 [16, 4096, 1024], P('users', 'cand'), may hold values from -6 to 6
- cand_key: bfloat16 [16, 4096, 1024], P('users', 'cand'), may hold values from -6 to 6
- cand_value: bfloat16 [16, 4096, 1024], P('users', 'cand'), may hold values from -6 to 6
- cand_gate: bfloat16 [16, 4096, 1024], P('users', 'cand'), may hold values from -6 to 6
- residual_in: bfloat16 [16, 4096, 1024], P('users', 'cand'), may hold values from -6 to 6
- hist_key: bfloat16 [16, 1024, 1024], P('users', 'cand'), may hold values from -6 to 6
- hist_value: bfloat16 [16, 1024, 1024], P('users', 'cand'), may hold values from -6 to 6
- micro_ids: int32 [16, 4096], P('users'), may hold values from 0 to 63, never falling along the last dimension, each value on 1 to 128 neighbouring positions
- pattern: int32 [128, 128], replicated, may hold values 0 or 1
- out_weight: bfloat16 [1024, 1024], P('cand', 'users'), may hold values from -0.1875 to 0.1875
Outputs:
- layer_out: bfloat16 [16, 4096, 1024], P('users', 'cand')
Inputs may be any that keep to these rules, and one draw needn't show every extreme that they name: `micro_ids`: in each row micro-batch numbers never fall; each micro-batch is a run of 1 to 128 consecutive candidates, and some run has exactly 128.
All inputs are finite; a program needn't handle non-finite values.
Results may differ from a plain program's by a relative error of at most 0.0051.
Values may be sent and summed in bfloat16 or wider, within the bound.
A program may use at most 64 MiB of HBM per device.

v0:
```python
import math

import jax
import jax.numpy as jnp
from jax import lax
from jax.sharding import PartitionSpec as P

H = 8
DH = 128
MB_MAX = 128


def from_behind(value, axis, steps):
    count = lax.axis_size(axis)
    leading, last = (max(0, -steps), min(count, count - steps))
    return lax.ppermute(value, axis, [(source, source + steps) for source in range(leading, last)])


def micro_offsets(ids_row):
    positions = jnp.arange(ids_row.shape[0], dtype=jnp.int32)
    boundary = jnp.concatenate([jnp.ones((1,), jnp.bool_), ids_row[1:] != ids_row[:-1]])
    starts = lax.cummax(jnp.where(boundary, positions, 0))
    return positions - starts


def history_adder(queries, head_count, factor, total, pieces):
    key_piece = pieces[0][0]
    value_piece = pieces[1][0]
    length = key_piece.shape[0]
    width = math.gcd(length, 512)

    def add_block(index_block, running):
        keys_block = lax.dynamic_slice_in_dim(key_piece, index_block * width, width, 0).reshape(
            width, head_count, DH
        )
        values_block = lax.dynamic_slice_in_dim(value_piece, index_block * width, width, 0).reshape(
            width, head_count, DH
        )
        scores = (
            jnp.einsum("rhd,khd->hrk", queries, keys_block, preferred_element_type=jnp.float32)
            * factor
        )
        weights = jax.nn.silu(scores).astype(jnp.bfloat16)
        return running + jnp.einsum(
            "hrk,khd->rhd", weights, values_block, preferred_element_type=jnp.float32
        )

    return lax.fori_loop(0, length // width, add_block, total)


def shards(
    cand_query,
    cand_key,
    cand_value,
    cand_gate,
    residual_in,
    hist_key,
    hist_value,
    micro_ids,
    pattern,
    out_weight,
):
    count = cand_query.shape[1]
    width_all = cand_query.shape[2]
    reach = MB_MAX - 1
    factor = DH ** (-0.5)
    rank = lax.axis_index("cand")
    ids_row = micro_ids[0]
    offsets = micro_offsets(ids_row)
    pad_ids = jnp.concatenate(
        [jnp.full((reach,), -1, jnp.int32), ids_row, jnp.full((reach,), -1, jnp.int32)]
    )
    pad_off = jnp.concatenate(
        [jnp.zeros((reach,), jnp.int32), offsets, jnp.zeros((reach,), jnp.int32)]
    )
    first_row = rank * count
    own_ids = lax.dynamic_slice_in_dim(ids_row, first_row, count, 0)
    own_off = lax.dynamic_slice_in_dim(offsets, first_row, count, 0)
    near_ids = lax.dynamic_slice_in_dim(pad_ids, first_row, count + 2 * reach, 0)
    near_off = lax.dynamic_slice_in_dim(pad_off, first_row, count + 2 * reach, 0)
    paired = jnp.concatenate([cand_key[0], cand_value[0]], axis=1)
    before = from_behind(paired, "cand", 1)
    after = from_behind(paired, "cand", -1)
    nearby = jnp.concatenate([before[count - reach :], paired, after[:reach]], axis=0)
    queries = cand_query[0].reshape(count, H, DH)
    pattern_float = pattern.astype(jnp.float32)
    slots = jnp.arange(MB_MAX, dtype=jnp.int32)
    block = min(count, 512)
    window = block + 2 * reach
    near_keys = nearby[:, :width_all].reshape(window, H, DH)
    near_values = nearby[:, width_all:].reshape(window, H, DH)
    onehot_rows = (own_off[:, None] == slots[None, :]).astype(jnp.float32)
    onehot_keys = (near_off[:, None] == slots[None, :]).astype(jnp.float32)
    lookup = jnp.dot(
        jnp.dot(onehot_rows, pattern_float, precision=lax.Precision.HIGHEST),
        onehot_keys.T,
        precision=lax.Precision.HIGHEST,
    )
    same = own_ids[:, None] == near_ids[None, :]
    diagonal = jnp.arange(block)[:, None] + reach == jnp.arange(window)[None, :]
    visible = same & ((lookup > 0.5) | diagonal)
    scores = (
        jnp.einsum("rhd,khd->hrk", queries, near_keys, preferred_element_type=jnp.float32) * factor
    )
    weights = jnp.where(visible[None], jax.nn.silu(scores), 0.0).astype(jnp.bfloat16)
    pieces_self = jnp.einsum(
        "hrk,khd->rhd", weights, near_values, preferred_element_type=jnp.float32
    )
    attended = pieces_self
    start_total = jnp.zeros((count, H, DH), jnp.float32)
    from_history = history_adder(
        queries,
        H,
        factor,
        start_total,
        (
            lax.all_gather(hist_key, "cand", axis=1, tiled=True),
            lax.all_gather(hist_value, "cand", axis=1, tiled=True),
        ),
    )
    attended = (attended + from_history).reshape(count, width_all)
    center = jnp.mean(attended, axis=1, keepdims=True)
    spread = jnp.mean((attended - center) ** 2, axis=1, keepdims=True)
    normed = (attended - center) * lax.rsqrt(spread + 1e-05)
    gated = (normed * cand_gate[0].astype(jnp.float32)).astype(jnp.bfloat16)
    columns = lax.all_gather(out_weight, "users", axis=1, tiled=True)
    projected = jnp.dot(
        gated,
        lax.all_gather(columns, "cand", axis=0, tiled=True),
        preferred_element_type=jnp.float32,
    )
    result = (residual_in[0].astype(jnp.float32) + projected).astype(jnp.bfloat16)
    return result[None]


def solution(mesh):
    placed = (
        P("users", "cand", None),
        P("users", "cand", None),
        P("users", "cand", None),
        P("users", "cand", None),
        P("users", "cand", None),
        P("users", "cand", None),
        P("users", "cand", None),
        P("users", None),
        P(),
        P("cand", "users"),
    )
    return jax.shard_map(
        shards, mesh=mesh, in_specs=placed, out_specs=P("users", "cand", None), check_vma=False
    )
```

profile of v0, /device:TPU:6, one launch (start us, length us, event | category | flops | bytes accessed | tf_op | source)
XLA Modules:
  0.0 704.7 jit_solution(15050172416284282905)
XLA Ops:
  6.5 0.0 copy-start.6
  6.5 0.0 all-gather.5.cloned.1.call-start
  6.5 0.7 all-gather.5.cloned.1.call-update
  7.3 0.0 all-gather.7.cloned.1.call-start
  7.3 0.7 all-gather.7.cloned.1.call-update
  8.0 0.0 all-gather.9.cloned.1.call-start
  8.1 1.1 pad_maximum_fusion.1
  9.1 0.0 copy-start
  9.1 0.0 copy-start.1
  9.2 4.0 collective-permute-start
  13.1 1.3 collective-permute-start.1
  14.4 46.9 %all-gather = bf16[16,64,32]{1,2,0:T(8,128)(2,1)S(1)} all-gather(bf16[1,64,32]{1,2,0:T(8,128)(2,1)} %bitcast.113), channel_id=1, replica_groups=mesh['users'=16,'cand'=32] {'users'}, dimensions={0}, use_global_device_ids=true | all-gather | bytes 69632 | tf_op jit(solution)/shard_map/all_gather | solution.py:126
  61.3 0.1 copy.57
  61.4 0.8 reshape.81
  62.1 0.0 all-gather.9.cloned.1.call-update
  62.2 0.9 compare_reduce_fusion
  63.1 0.1 add_select_fusion
  63.2 0.3 reduce-window.9
  63.5 0.1 slice.38
  63.5 0.1 reduce-window.12
  63.6 0.1 slice_reduce_fusion
  63.7 0.1 bitcast_subtract_fusion
  63.8 0.1 dynamic_slice.28
  63.9 0.1 concatenate.22
  64.0 0.1 dynamic_slice.29
  64.0 0.0 copy-done.5
  64.0 0.1 concatenate.19
  64.1 0.1 dynamic_slice.27
  64.2 0.0 copy-done.6
  64.2 0.2 fusion.26
  64.4 0.4 fusion.18
  64.8 0.2 copy.46
  65.0 0.0 copy-done.4
  65.0 0.2 copy.48
  65.2 0.2 copy.55
  65.4 0.0 collective-permute-done
  65.4 0.1 slice.35
  65.5 0.0 collective-permute-done.1
  65.5 0.0 copy-done
  65.5 0.0 copy-done.1
  65.5 0.3 pad_maximum_fusion
  65.9 0.1 fusion.29
  66.0 0.4 copy.47
  66.4 1.1 copy.45
  67.5 0.4 fusion.31
  67.9 2.2 fusion.13
  70.1 175.4 %all-gather.5.cloned.1.call-done = bf16[1,1024,1024]{2,1,0:T(8,128)(2,1)} async-done(((bf16[1,32,1024]{2,1,0:T(8,128)(2,1)}), bf16[1,1024,1024]{2,1,0:T(8,128)(2,1)}) %all-gather.5.cloned.1.call-update) | async-done | bytes 2097168 | tf_op jit(solution)/shard_map/all_gather | solution.py:118
  245.5 222.4 %all-gather.7.cloned.1.call-done = bf16[1,1024,1024]{2,1,0:T(8,128)(2,1)} async-done(((bf16[1,32,1024]{2,1,0:T(8,128)(2,1)}), bf16[1,1024,1024]{2,1,0:T(8,128)(2,1)}) %all-gather.7.cloned.1.call-update) | async-done | bytes 2097168 | tf_op jit(solution)/shard_map/all_gather | solution.py:117
  467.9 10.7 %while.14 = (s32[]{:T(128)}, f32[128,8,128]{0,2,1:T(8,128)}, bf16[1024,1024]{1,0:T(8,128)(2,1)}, bf16[1024,1024]{1,0:T(8,128)(2,1)}, bf16[128,8,128]{2,0,1:T(8,1...) while((s32[]{:T(128)}, f32[128,8,128]{0,2,1:T(8,128)}, ...), condition=%wide.region_3.4_spmd.clone, body=%wide.region_2.3_spmd.clone.sunk | while | flops 271843328 | bytes 11796633 | solution.py:48
  467.9 1.7 constant_dynamic-slice_fusion.3
  469.6 0.5 copy.75
  470.1 0.5 copy.76
  470.7 2.0 fusion.47
  472.7 1.7 constant_dynamic-slice_fusion.3
  474.4 0.5 copy.75
  475.0 0.5 copy.76
  475.5 3.0 fusion.47
  478.5 2.0 fusion.30
  480.5 0.2 copy.56
  480.7 0.2 multiply_reduce_fusion
  480.9 214.4 %all-gather.9.cloned.1.call-done = bf16[1024,1024]{1,0:T(8,128)(2,1)} async-done(((bf16[32,1024]{1,0:T(8,128)(2,1)}), bf16[1024,1024]{1,0:T(8,128)(2,1)}) %all-gather.9.cloned.1.call-update) | async-done | bytes 2097168 | tf_op jit(solution)/shard_map/all_gather | solution.py:129
  695.3 0.0 copy-done.2
  695.3 0.0 copy-done.3
  695.3 2.8 fusion.16
  (11 shorter events, 0.0 us)
Async XLA Ops:
  6.5 57.5 %copy-start.5 = (s32[1,4096]{1,0:T(1,128)S(1)}, s32[1,4096]{1,0:T(1,128)}, u32[]{:S(2)}) copy-start(s32[1,4096]{1,0:T(1,128)} %param.19) | copy-start | bytes 49156
  6.5 57.7 %copy-start.6 = (s32[128,128]{1,0:T(8,128)S(1)}, s32[128,128]{1,0:T(8,128)}, u32[]{:S(2)}) copy-start(s32[128,128]{1,0:T(8,128)} %param.20) | copy-start | bytes 196612
  6.5 58.4 %copy-start.4 = (bf16[1,128,1024]{2,1,0:T(8,128)(2,1)S(1)}, bf16[1,128,1024]{2,1,0:T(8,128)(2,1)}, u32[]{:S(2)}) copy-start(bf16[1,128,1024]{2,1,0:T(8,128)(2,1)} %param.12) | copy-start | bytes 786436
  6.5 239.0 %all-gather.5.cloned.1.call-start = ((), (), s32[]{:S(2)}) async-start(), calls=%async_computation | async-start | bytes 2162688 | tf_op jit(solution)/shard_map/all_gather | solution.py:118
  7.3 460.6 %all-gather.7.cloned.1.call-start = ((), (), s32[]{:S(2)}) async-start(), calls=%async_computation.1 | async-start | bytes 2162688 | tf_op jit(solution)/shard_map/all_gather | solution.py:117
  8.0 687.3 %all-gather.9.cloned.1.call-start = ((), (), s32[]{:S(2)}) async-start(), calls=%async_computation.2 | async-start | bytes 2162688 | tf_op jit(solution)/shard_map/all_gather | solution.py:129
  9.1 56.4 %copy-start = (bf16[1,128,1024]{2,1,0:T(8,128)(2,1)S(1)}, bf16[1,128,1024]{2,1,0:T(8,128)(2,1)}, u32[]{:S(2)}) copy-start(bf16[1,128,1024]{2,1,0:T(8,128)(2,1)} %param.14) | copy-start | bytes 786436
  9.1 56.4 %copy-start.1 = (bf16[1,128,1024]{2,1,0:T(8,128)(2,1)S(1)}, bf16[1,128,1024]{2,1,0:T(8,128)(2,1)}, u32[]{:S(2)}) copy-start(bf16[1,128,1024]{2,1,0:T(8,128)(2,1)} %param.13) | copy-start | bytes 786436
  9.2 56.2 %collective-permute-start = (bf16[128,2048]{1,0:T(8,128)(2,1)S(1)}, bf16[128,2048]{1,0:T(8,128)(2,1)S(1)}, u32[]{:S(2)}, u32[]{:S(2)}) collective-permute-start(bf16[128,2048]{1,0:T(8,128)(2,1)S(1)} %pad_maximum_fusion.1), channel_id=1, source_target_pairs={{0,1},{1,2},{2,3},{3,4},{4,5},{5,6},{6,7},{7,8},{8,9},{9,10},{10,1... | collective-permute-start | bytes 1572872 | tf_op jit(solution)/shard_map/ppermute | solution.py:16
  13.1 52.4 %collective-permute-start.1 = (bf16[128,2048]{1,0:T(8,128)(2,1)S(1)}, bf16[128,2048]{1,0:T(8,128)(2,1)S(1)}, u32[]{:S(2)}, u32[]{:S(2)}) collective-permute-start(bf16[128,2048]{1,0:T(8,128)(2,1)S(1)} %pad_maximum_fusion.1), channel_id=1, source_target_pairs={{1,0},{2,1},{3,2},{4,3},{5,4},{6,5},{7,6},{8,7},{9,8},{10,9},{11,1... | collective-permute-start | bytes 1572872 | tf_op jit(solution)/shard_map/ppermute | solution.py:16
  478.5 216.8 %copy-start.2 = (bf16[1,128,1024]{2,1,0:T(8,128)(2,1)S(1)}, bf16[1,128,1024]{2,1,0:T(8,128)(2,1)}, u32[]{:S(2)}) copy-start(bf16[1,128,1024]{2,1,0:T(8,128)(2,1)} %param.15) | copy-start | bytes 786436
  478.5 216.8 %copy-start.3 = (bf16[1,128,1024]{2,1,0:T(8,128)(2,1)S(1)}, bf16[1,128,1024]{2,1,0:T(8,128)(2,1)}, u32[]{:S(2)}) copy-start(bf16[1,128,1024]{2,1,0:T(8,128)(2,1)} %param.16) | copy-start | bytes 786436
Sparse Core Ops, SparseCore 0:
  9.4 236.0 all-gather.4
  247.6 220.2 all-gather.6
  470.0 225.3 all-gather.8
where the time goes:
time: 705 us
  waiting for transfers between devices  614 us (87%)
  blocking collectives  46.9 us (7%)
  between operations  13.3 us (2%)
  matrix products  10.8 us (2%)
  local copies, waits for them, and re-layouts  9.53 us (1%)
    all_gather x1, waiting for transfers between devices, shards(): lax.all_gather(hist_key, 'cand', axis=1, tiled=True)  222 us
    all_gather x1, waiting for transfers between devices, shards(): lax.all_gather(columns, 'cand', axis=0, tiled=True)  214 us
    all_gather x1, waiting for transfers between devices, shards(): lax.all_gather(hist_value, 'cand', axis=1, tiled=True)  175 us
    all_gather x1, blocking collectives, shards(): columns = lax.all_gather(out_weight, 'users', axis=1, tiled=True)  46.9 us
  transfers between devices with their start and end apart: 5, of which 3 were waited for; matrix products, arithmetic and copies ran while one was open for 3% of the time, Pallas kernels for 0%

commit v1 on v0

v1 whole, which is shorter than its diff:
```python
import jax
import jax.numpy as jnp
from jax import lax
from jax.experimental import pallas as pl
from jax.experimental.pallas import tpu as pltpu
from jax.sharding import PartitionSpec as P

H = 8
DH = 128
NX, NZH, NCORE = 4, 2, 2
NY, NZL = 4, 8
NCAND = NY * NZL
HEADS = H // NY
SHARE = HEADS * DH
MESH = pl.DeviceIdType.MESH
BF16, F32 = jnp.bfloat16, jnp.float32


def dot(a, b):
    return lax.dot_general(a, b, (((1,), (0,)), ((), ())), preferred_element_type=F32)


def dot_t(a, b):
    return lax.dot_general(a, b, (((1,), (1,)), ((), ())), preferred_element_type=F32)


def silu_of_half(h):
    return (h + h * jnp.tanh(h)).astype(BF16)


def kernel(
    q_hbm, k_hbm, v_hbm, gate_hbm, res_hbm, hk_hbm, hv_hbm, ids_hbm, pat_hbm, w_hbm,
    out_ref,
    rows5, ids_ref, pat_ref, w_ref,
    kvh, qh, oh, part_out, part_in, halo, wtmp, wb, maskh, att,
    in_sem, kv_recv, own_send, z_send, ys_send, ys_recv, o_send, o_recv, halo_send, halo_recv,
    wc_send, wc_recv, wz_send, wz_recv, wy_send, wy_recv, wx_send, wx_recv, wo_send, wo_recv,
):
    u, c = lax.axis_index("users"), lax.axis_index("cand")
    core = lax.rem(u, NCORE)
    zh = lax.rem(u // NCORE, NZH)
    x = u // (NCORE * NZH)
    z = lax.rem(c, NZL)
    y = c // NZL
    rows = q_hbm.shape[0]
    q_ref, k_ref, v_ref, gate_ref, res_ref = [rows5.at[i] for i in range(5)]

    def share(y_):
        return pl.ds(pl.multiple_of(y_ * SHARE, SHARE), SHARE)

    incoming = [
        pltpu.make_async_copy(src, dst, in_sem.at[i])
        for i, (src, dst) in enumerate([
            (w_hbm, w_ref), (ids_hbm, ids_ref), (pat_hbm, pat_ref),
            (hk_hbm.at[:, share(y)], kvh.at[z, 0, y]), (hv_hbm.at[:, share(y)], kvh.at[z, 1, y]),
            (q_hbm.at[:, share(y)], qh.at[y]),
            (q_hbm, q_ref), (k_hbm, k_ref), (v_hbm, v_ref), (gate_hbm, gate_ref), (res_hbm, res_ref),
        ])
    ]
    for copy in incoming:
        copy.start()

    def dev(x_, zh_, core_, y_, z_):
        return {"users": (x_ * NZH + zh_) * NCORE + core_, "cand": y_ * NZL + z_}

    def on_cand(c_):
        return {"users": u, "cand": c_}

    def along_z(d):
        far = lax.rem(zh * NZL + z + d, NZH * NZL)
        return far // NZL, lax.rem(far, NZL)

    other_core = dev(x, zh, 1 - core, y, z)
    nxt, prv = lax.rem(c + 1, NCAND), lax.rem(c + NCAND - 1, NCAND)

    barrier = pltpu.get_barrier_semaphore()

    def greet(device):
        pl.semaphore_signal(barrier, inc=1, device_id=device, device_id_type=MESH)

    for d in range(1, NZH * NZL):
        zh_, z_ = along_z(d)
        greet(dev(x, zh_, core, y, z_))
    for d in range(1, NY):
        greet(dev(x, zh, core, lax.rem(y + d, NY), z))
    for d in range(1, NX):
        greet(dev(lax.rem(x + d, NX), zh, core, y, z))
    greet(other_core)

    @pl.when(z == NZL - 1)
    def _():
        greet(on_cand(nxt))

    @pl.when(z == 0)
    def _():
        greet(on_cand(prv))

    partners = NZH * NZL - 1 + NY - 1 + NX - 1 + 1
    edge = jnp.where(z == 0, 1, 0) + jnp.where(z == NZL - 1, 1, 0)
    pl.semaphore_wait(barrier, partners + edge)

    def remote(src, dst, send, recv, device):
        return pltpu.make_async_remote_copy(
            src_ref=src, dst_ref=dst, send_sem=send, recv_sem=recv,
            device_id=device, device_id_type=MESH,
        )

    def z_of(t):
        both = 2 * jnp.minimum(z, NZL - 1 - z)
        turn = z - (t + 1) // 2 if t % 2 else z + t // 2
        return jnp.where(t <= both, turn, jnp.where(2 * z < NZL, t, NZL - 1 - t))

    def to_head(i, d):
        y_ = lax.rem(y + d, NY)
        src = (hk_hbm, hv_hbm, q_hbm)[i].at[:, share(y_)]
        dst = qh.at[y] if i == 2 else kvh.at[z, i, y]
        return remote(src, dst, ys_send.at[i, d - 1], ys_recv.at[i, d - 1], on_cand(y_ * NZL + z))

    def at_head(i, d):
        y_ = lax.rem(y + NY - d, NY)
        here = qh.at[y_] if i == 2 else kvh.at[z, i, y_]
        remote(here, here, ys_send.at[0, 0], ys_recv.at[i, d - 1], other_core).wait_recv()

    def from_head(d):
        y_ = lax.rem(y + d, NY)
        return remote(part_out.at[y_], part_in.at[y], o_send.at[d - 1], o_recv.at[d - 1], on_cand(y_ * NZL + z))

    def back_home(d):
        here = part_in.at[lax.rem(y + NY - d, NY)]
        remote(here, here, o_send.at[0], o_recv.at[d - 1], other_core).wait_recv()

    def own_z(a, way):
        to = on_cand(y * NZL + (z + 1 if way == 0 else z - 1))
        return remote(kvh.at[z, a], kvh.at[z, a], own_send.at[way, a], kv_recv.at[a, z], to)

    def hop_z(a, z_):
        to = on_cand(y * NZL + z + jnp.where(z_ < z, 1, -1))
        return remote(kvh.at[z_, a], kvh.at[z_, a], z_send.at[a, z_], kv_recv.at[a, z_], to)

    def goes_on(z_):
        return ((z_ < z) & (z < NZL - 1)) | ((z_ > z) & (z > 0))

    def arrived(a, z_):
        here = kvh.at[z_, a]
        remote(here, here, own_send.at[0, 0], kv_recv.at[a, z_], other_core).wait_recv()

    def halo_copy(way, a):
        return remote(
            (k_hbm, v_hbm)[a], halo.at[way, a], halo_send.at[way, a], halo_recv.at[way, a],
            on_cand(nxt if way == 0 else prv),
        )

    tile_core = remote(w_hbm, wtmp, wc_send, wc_recv, other_core)

    def tile_z(d):
        zh_, z_ = along_z(d)
        here = wb.at[core, x, y, z]
        return remote(here, here, wz_send.at[d - 1], wz_recv.at[z], dev(x, zh_, core, y, z_))

    def tile_y(d):
        here = wb.at[core, x, y]
        return remote(here, here, wy_send.at[d - 1], wy_recv.at[d - 1], dev(x, zh, core, lax.rem(y + d, NY), z))

    def tile_x(d):
        here = wb.at[core, x]
        return remote(here, here, wx_send.at[d - 1], wx_recv.at[d - 1], dev(lax.rem(x + d, NX), zh, core, y, z))

    def tile_out(d):
        here = wb.at[core, lax.rem(x + d, NX)]
        return remote(here, here, wo_send.at[d], wo_recv.at[d], other_core)

    for i in range(3):
        for d in range(1, NY):
            to_head(i, d).start()
    tile_core.start()

    for copy in incoming[:3]:
        copy.wait()

    def ids_row(b):
        at = jnp.clip(b, 0, NCAND - 1) * DH
        got = ids_ref[:, pl.ds(pl.multiple_of(at, DH), DH)].astype(F32)
        return jnp.where((b >= 0) & (b < NCAND), got, -1.0)

    square = (rows, rows)
    sub = lax.broadcasted_iota(jnp.int32, square, 0)
    lane = lax.broadcasted_iota(jnp.int32, square, 1)
    half_factor = 0.5 * DH ** (-0.5)

    def make_mask():
        ids = [ids_row(c + d) for d in (-2, -1, 0, 1)]
        wide = [jnp.broadcast_to(r, square) for r in ids]
        tall = [w.T for w in wide]
        offs = []
        for b in (1, 2, 3):
            whole = jnp.where(tall[b - 1] == wide[b], 1.0, 0.0)
            part = jnp.where((tall[b] == wide[b]) & (sub < lane), 1.0, 0.0)
            offs.append(jnp.sum(whole + part, axis=0, keepdims=True))
        own_off = jnp.broadcast_to(offs[1], square).T
        hot_rows = jnp.where(own_off == lane.astype(F32), 1.0, 0.0).astype(BF16)
        allowed = jnp.where(pat_ref[...] == 1, 1.0, 0.0).astype(BF16)
        by_row = dot(hot_rows, allowed).astype(BF16)
        for b in range(3):
            hot_keys = jnp.where(sub.astype(F32) == jnp.broadcast_to(offs[b], square), 1.0, 0.0).astype(BF16)
            seen = dot(by_row, hot_keys) > 0.5
            if b == 1:
                seen = seen | (sub == lane)
            seen = seen & (tall[2] == wide[b + 1])
            maskh[b] = jnp.where(seen, half_factor, 0.0)

    for copy in incoming[3:5]:
        copy.wait()
    for a in range(2):
        for d in range(1, NY):
            at_head(a, d)

        @pl.when(z < NZL - 1)
        def _():
            own_z(a, 0).start()

        @pl.when(z > 0)
        def _():
            own_z(a, 1).start()

    tile_core.wait()
    mine, theirs = w_ref[...].astype(F32), wtmp[...].astype(F32)
    tile = jnp.where(
        core == 0, jnp.concatenate([mine, theirs], axis=1), jnp.concatenate([theirs, mine], axis=1)
    ).astype(BF16)

    @pl.when(core == zh)
    def _():
        wb[core, x, y, z] = tile
        for d in range(1, NZH * NZL):
            tile_z(d).start()

    make_mask()

    def own_chunk():
        for copy in incoming[6:9]:
            copy.wait()
        for h in range(H):
            cols = slice(h * DH, (h + 1) * DH)
            weights = silu_of_half(dot_t(q_ref[:, cols], k_ref[:, cols]) * maskh[1])
            att[:, cols] = dot(weights, v_ref[:, cols])

    def halo_chunk(way):
        for a in range(2):
            halo_copy(way, a).wait_recv()
        for h in range(H):
            cols = slice(h * DH, (h + 1) * DH)
            weights = silu_of_half(dot_t(q_ref[:, cols], halo[way, 0, :, cols]) * maskh[2 * way])
            att[:, cols] = att[:, cols] + dot(weights, halo[way, 1, :, cols])

    def hist_chunk(t):
        z_ = z_of(t)
        if t == 0:
            incoming[5].wait()
            for d in range(1, NY):
                at_head(2, d)
        for h in range(HEADS):
            cols = slice(h * DH, (h + 1) * DH)
            keys = kvh[z_, 0, :, :, cols].reshape(-1, DH)
            values = kvh[z_, 1, :, :, cols].reshape(-1, DH)
            weights = silu_of_half(dot_t(qh[:, :, cols].reshape(-1, DH), keys) * half_factor)
            more = dot(weights, values)
            oh[h] = more if t == 0 else oh[h] + more

    halo_at = {1: [(0, 0)], 3: [(0, 1)], 5: [(1, 0)], 7: [(1, 1)]}
    for t in range(1, NZL):
        z_ = z_of(t)
        for a in range(2):
            arrived(a, z_)

            @pl.when(goes_on(z_))
            def _():
                hop_z(a, z_).start()

        for way, a in halo_at.get(t, []):
            halo_copy(way, a).start()
        if t == 1:
            own_chunk()
        if t == 2:
            for z_ in range(NZL):
                @pl.when((core != zh) | (z != z_))
                def _():
                    there = wb.at[core, x, y, z_]
                    remote(there, there, wz_send.at[0], wz_recv.at[z_], other_core).wait_recv()
            for d in range(1, NY):
                tile_y(d).start()
        if t == 4:
            for d in range(1, NY):
                there = wb.at[core, x, lax.rem(y + NY - d, NY)]
                remote(there, there, wy_send.at[0], wy_recv.at[d - 1], other_core).wait_recv()
            for d in range(1, NX):
                tile_x(d).start()
            tile_out(0).start()
        hist_chunk(t - 1)
    hist_chunk(NZL - 1)
    for y_ in range(NY):
        for h in range(HEADS):
            part_out[y_, :, h * DH:(h + 1) * DH] = oh[h, y_ * rows:(y_ + 1) * rows].astype(BF16)
    for d in range(1, NY):
        from_head(d).start()
    part_in[y] = part_out[y]
    for d in range(1, NX):
        there = wb.at[core, lax.rem(x + NX - d, NX)]
        remote(there, there, wx_send.at[0], wx_recv.at[d - 1], other_core).wait_recv()
        tile_out(NX - d).start()
    halo_chunk(0)
    halo_chunk(1)

    for copy in incoming[9:]:
        copy.wait()
    for d in range(1, NY):
        back_home(d)
    for y_ in range(NY):
        cols = slice(y_ * SHARE, (y_ + 1) * SHARE)
        att[:, cols] = att[:, cols] + part_in[y_].astype(F32)
    attended = att[...]
    center = jnp.mean(attended, axis=1, keepdims=True)
    moved = attended - center
    spread = jnp.mean(moved * moved, axis=1, keepdims=True)
    gated = (moved * lax.rsqrt(spread + 1e-05) * gate_ref[...].astype(F32)).astype(BF16)

    for d in range(NX):
        there = wb.at[1 - core, lax.rem(x + d, NX)]
        remote(there, there, wo_send.at[0], wo_recv.at[d], other_core).wait_recv()
    for x_ in range(NX):
        cols = slice(x_ * 2 * DH, (x_ + 1) * 2 * DH)
        weight = jnp.concatenate(
            [wb[0, x_].reshape(-1, DH), wb[1, x_].reshape(-1, DH)], axis=1
        )
        out_ref[:, cols] = (res_ref[:, cols].astype(F32) + dot(gated, weight)).astype(BF16)

    @pl.when(z < NZL - 1)
    def _():
        for a in range(2):
            own_z(a, 0).wait_send()

    @pl.when(z > 0)
    def _():
        for a in range(2):
            own_z(a, 1).wait_send()

    for t in range(1, NZL):
        z_ = z_of(t)

        @pl.when(goes_on(z_))
        def _():
            for a in range(2):
                hop_z(a, z_).wait_send()

    for d in range(1, NY):
        for i in range(3):
            to_head(i, d).wait_send()
        from_head(d).wait_send()
    for way in range(2):
        for a in range(2):
            halo_copy(way, a).wait_send()

    @pl.when(core == zh)
    def _():
        for d in range(1, NZH * NZL):
            tile_z(d).wait_send()

    for d in range(1, NY):
        tile_y(d).wait_send()
    for d in range(1, NX):
        tile_x(d).wait_send()
    for d in range(NX):
        tile_out(d).wait_send()


def shards(q, k, v, gate, resid, hk, hv, ids, pattern, weight):
    rows, width = q.shape[1:]
    hist = hk.shape[1]
    hbm = pl.BlockSpec(memory_space=pl.ANY)
    vmem = pl.BlockSpec(memory_space=pltpu.VMEM)
    dma = pltpu.SemaphoreType.DMA
    out = pl.pallas_call(
        kernel,
        out_shape=jax.ShapeDtypeStruct((rows, width), BF16),
        in_specs=[hbm] * 10,
        out_specs=vmem,
        scratch_shapes=[
            pltpu.VMEM((5, rows, width), BF16),
            pltpu.VMEM(ids.shape, ids.dtype),
            pltpu.VMEM(pattern.shape, pattern.dtype),
            pltpu.VMEM(weight.shape, BF16),
            pltpu.VMEM((NZL, 2, NY, hist, SHARE), BF16),
            pltpu.VMEM((NY, rows, SHARE), BF16),
            pltpu.VMEM((HEADS, NY * rows, DH), F32),
            pltpu.VMEM((NY, rows, SHARE), BF16),
            pltpu.VMEM((NY, rows, SHARE), BF16),
            pltpu.VMEM((2, 2, rows, width), BF16),
            pltpu.VMEM(weight.shape, BF16),
            pltpu.VMEM((NZH, NX, NY, NZL, weight.shape[0], 2 * weight.shape[1]), BF16),
            pltpu.VMEM((3, rows, rows), F32),
            pltpu.VMEM((rows, width), F32),
            dma((11,)), dma((2, NZL)), dma((2, 2)), dma((2, NZL)), dma((3, NY - 1)), dma((3, NY - 1)),
            dma((NY - 1,)), dma((NY - 1,)), dma((2, 2)), dma((2, 2)),
            dma, dma, dma((NZH * NZL - 1,)), dma((NZL,)), dma((NY - 1,)), dma((NY - 1,)),
            dma((NX - 1,)), dma((NX - 1,)), dma((NX,)), dma((NX,)),
        ],
        compiler_params=pltpu.CompilerParams(
            collective_id=0, has_side_effects=True, vmem_limit_bytes=60 * 1024 * 1024
        ),
    )(q[0], k[0], v[0], gate[0], resid[0], hk[0], hv[0], ids, pattern, weight)
    return out[None]


def solution(mesh):
    part = P("users", "cand", None)
    return jax.shard_map(
        shards,
        mesh=mesh,
        in_specs=(part,) * 7 + (P("users", None), P(), P("cand", "users")),
        out_specs=part,
        check_vma=False,
    )
```

time: 705 us -> 75 us (0.11)
  waiting for transfers between devices: 614 us -> 0 us
  Pallas kernels: 0 us -> 73.2 us
  blocking collectives: 46.9 us -> 0 us
  between operations: 13.3 us -> 0.01 us
  matrix products: 10.8 us -> 0 us
  local copies, waits for them, and re-layouts: 9.53 us -> 1.67 us
    all_gather x3 -> x0, waiting for transfers between devices: 612 us -> none  [the longest x1 222 us: shards(): lax.all_gather(hist_key, 'cand', axis=1, tiled=True)]
    pallas_call x0 -> x1, Pallas kernels: none -> 73.2 us  [shards(): pl.pallas_call(kernel, out_shape=jax.ShapeDtypeStruct((rows, width), BF16...]
    all_gather x1 -> x0, blocking collectives: 46.9 us -> none  [shards(): columns = lax.all_gather(out_weight, 'users', axis=1, tiled=True)]
    dot_general x7 -> x0, matrix products: 10.8 us -> none  [the longest x2 5.01 us: add_block(): jnp.einsum('hrk,khd->rhd', weights, values_block, preferred_element_type=...]
  transfers between devices with their start and end apart: 5 -> 0, of which waited for: 3 -> 0; matrix products, arithmetic and copies ran while one was open for 3% -> 0% of each run, Pallas kernels for 0% -> 0%
where the time goes in v1:
time: 75 us; the launch traced here: 74.8 us
  Pallas kernels  73.2 us (98%)
  local copies, waits for them, and re-layouts  1.67 us (2%)
    pallas_call x1, Pallas kernels, shards(): pl.pallas_call(kernel, out_shape=jax.ShapeDtypeStruct((rows, width), BF16...  73.2 us
    unnamed x1, local copies, waits for them, and re-layouts  1.67 us

profile of v1, /device:TPU:6, one launch (start us, length us, event | category | flops | bytes accessed | tf_op | source)
XLA Modules:
  0.0 74.8 jit_solution(5296021633260464846)
XLA Ops:
  0.0 73.2 %shard_map.100 = bf16[128,1024]{1,0:T(8,128)(2,1)} custom-call(bf16[128,1024]{1,0:T(8,128)(2,1)} %bitcast.9, bf16[128,1024]{1,0:T(8,128)(2,1)} %bitcast.10, bf16[128,1024]{1,0:T(8,128)(2,1)} %bitcast.11, bf16[128,1024]{1,0:T(8,128)(2,1)} %bitcast.12, bf16[128,1024]{1,0:T(8,128)(2,1)} %bitcast.13, bf16[32,1024]{1,0:T(8,128)(2,1)} %bitcast.14, ...), custom_call_target="tpu_custom_call" | custom-call | tf_op jit(solution)/shard_map/pallas_call | solution.py:381
  73.2 1.7 %copy.12 = bf16[1,128,1024]{2,1,0:T(8,128)(2,1)} copy(bf16[1,128,1024]{2,1,0:T(8,128)(2,1)} %bitcast.8) | data formatting | bytes 524288

commit v2 on v1

--- a/solution.py
+++ b/solution.py
@@ -172,6 +172,7 @@
     for i in range(3):
         for d in range(1, NY):
             to_head(i, d).start()
+    halo_copy(0, 0).start()
     tile_core.start()
 
     for copy in incoming[:3]:
@@ -266,7 +267,7 @@
             more = dot(weights, values)
             oh[h] = more if t == 0 else oh[h] + more
 
-    halo_at = {1: [(0, 0)], 3: [(0, 1)], 5: [(1, 0)], 7: [(1, 1)]}
+    halo_at = {1: [(1, 0)], 3: [(0, 1)], 5: [(1, 1)]}
     for t in range(1, NZL):
         z_ = z_of(t)
         for a in range(2):

time: 75 us -> 76.9 us (1.025)
  Pallas kernels: 73.2 us -> 75 us
    pallas_call x1, Pallas kernels: 73.2 us -> 75 us  [shards(): pl.pallas_call(kernel, out_shape=jax.ShapeDtypeStruct((rows, width), BF16...]
where the time goes in v2:
time: 76.9 us; the launch traced here: 76.7 us
  Pallas kernels  75 us (98%)
  local copies, waits for them, and re-layouts  1.67 us (2%)
    pallas_call x1, Pallas kernels, shards(): pl.pallas_call(kernel, out_shape=jax.ShapeDtypeStruct((rows, width), BF16...  75 us
    unnamed x1, local copies, waits for them, and re-layouts  1.67 us

profile of v2, /device:TPU:6, one launch (start us, length us, event | category | flops | bytes accessed | tf_op | source)
XLA Modules:
  0.0 76.7 jit_solution(7095072786209874184)
XLA Ops:
  0.0 75.0 %shard_map.100 = bf16[128,1024]{1,0:T(8,128)(2,1)} custom-call(bf16[128,1024]{1,0:T(8,128)(2,1)} %bitcast.9, bf16[128,1024]{1,0:T(8,128)(2,1)} %bitcast.10, bf16[128,1024]{1,0:T(8,128)(2,1)} %bitcast.11, bf16[128,1024]{1,0:T(8,128)(2,1)} %bitcast.12, bf16[128,1024]{1,0:T(8,128)(2,1)} %bitcast.13, bf16[32,1024]{1,0:T(8,128)(2,1)} %bitcast.14, ...), custom_call_target="tpu_custom_call" | custom-call | tf_op jit(solution)/shard_map/pallas_call | solution.py:382
  75.0 1.7 %copy.12 = bf16[1,128,1024]{2,1,0:T(8,128)(2,1)} copy(bf16[1,128,1024]{2,1,0:T(8,128)(2,1)} %bitcast.8) | data formatting | bytes 524288

commit v3 on v1

--- a/solution.py
+++ b/solution.py
@@ -32,7 +32,7 @@
     q_hbm, k_hbm, v_hbm, gate_hbm, res_hbm, hk_hbm, hv_hbm, ids_hbm, pat_hbm, w_hbm,
     out_ref,
     rows5, ids_ref, pat_ref, w_ref,
-    kvh, qh, oh, part_out, part_in, halo, wtmp, wb, maskh, att,
+    kvh, qh, oh, part_out, part_in, halo, far_out, far_in, wtmp, wb, maskh, att,
     in_sem, kv_recv, own_send, z_send, ys_send, ys_recv, o_send, o_recv, halo_send, halo_recv,
     wc_send, wc_recv, wz_send, wz_recv, wy_send, wy_recv, wx_send, wx_recv, wo_send, wo_recv,
 ):
@@ -144,11 +144,23 @@
         here = kvh.at[z_, a]
         remote(here, here, own_send.at[0, 0], kv_recv.at[a, z_], other_core).wait_recv()
 
+    outer = (z <= 1, z >= NZL - 2)
+    inner = ((z == NZL - 3) | (z == NZL - 2), (z == 1) | (z == 2))
+    wraps = (z == NZL - 1, z == 0)
+
     def halo_copy(way, a):
-        return remote(
-            (k_hbm, v_hbm)[a], halo.at[way, a], halo_send.at[way, a], halo_recv.at[way, a],
-            on_cand(nxt if way == 0 else prv),
-        )
+        src = (k_hbm, v_hbm, q_hbm, far_out.at[way])[a]
+        dst = far_in.at[way] if a == 3 else halo.at[way, a]
+        return remote(src, dst, halo_send.at[way, a], halo_recv.at[way, a], on_cand(nxt if way == 0 else prv))
+
+    def near_copies(kinds, when):
+        for way in range(2):
+            @pl.when(when[way])
+            def _():
+                for a in kinds:
+                    halo_copy(way, a).start()
+
+    plain = [~inner[way] & ~wraps[way] for way in range(2)]
 
     tile_core = remote(w_hbm, wtmp, wc_send, wc_recv, other_core)
 
@@ -172,6 +184,8 @@
     for i in range(3):
         for d in range(1, NY):
             to_head(i, d).start()
+    near_copies([0], wraps)
+    near_copies([2], outer)
     tile_core.start()
 
     for copy in incoming[:3]:
@@ -196,17 +210,23 @@
             whole = jnp.where(tall[b - 1] == wide[b], 1.0, 0.0)
             part = jnp.where((tall[b] == wide[b]) & (sub < lane), 1.0, 0.0)
             offs.append(jnp.sum(whole + part, axis=0, keepdims=True))
-        own_off = jnp.broadcast_to(offs[1], square).T
-        hot_rows = jnp.where(own_off == lane.astype(F32), 1.0, 0.0).astype(BF16)
         allowed = jnp.where(pat_ref[...] == 1, 1.0, 0.0).astype(BF16)
-        by_row = dot(hot_rows, allowed).astype(BF16)
-        for b in range(3):
-            hot_keys = jnp.where(sub.astype(F32) == jnp.broadcast_to(offs[b], square), 1.0, 0.0).astype(BF16)
-            seen = dot(by_row, hot_keys) > 0.5
-            if b == 1:
+
+        def of_rows(b):
+            off = jnp.broadcast_to(offs[b], square).T
+            return dot(jnp.where(off == lane.astype(F32), 1.0, 0.0).astype(BF16), allowed).astype(BF16)
+
+        by_row = [of_rows(b) for b in range(3)]
+        hot_keys = [
+            jnp.where(sub.astype(F32) == jnp.broadcast_to(offs[b], square), 1.0, 0.0).astype(BF16)
+            for b in range(3)
+        ]
+        for i, (r, b) in enumerate([(1, 0), (1, 1), (1, 2), (0, 1), (2, 1)]):
+            seen = dot(by_row[r], hot_keys[b]) > 0.5
+            if r == b:
                 seen = seen | (sub == lane)
-            seen = seen & (tall[2] == wide[b + 1])
-            maskh[b] = jnp.where(seen, half_factor, 0.0)
+            seen = seen & (tall[r + 1] == wide[b + 1])
+            maskh[i] = jnp.where(seen, half_factor, 0.0)
 
     for copy in incoming[3:5]:
         copy.wait()
@@ -244,13 +264,34 @@
             weights = silu_of_half(dot_t(q_ref[:, cols], k_ref[:, cols]) * maskh[1])
             att[:, cols] = dot(weights, v_ref[:, cols])
 
-    def halo_chunk(way):
-        for a in range(2):
-            halo_copy(way, a).wait_recv()
-        for h in range(H):
-            cols = slice(h * DH, (h + 1) * DH)
-            weights = silu_of_half(dot_t(q_ref[:, cols], halo[way, 0, :, cols]) * maskh[2 * way])
-            att[:, cols] = att[:, cols] + dot(weights, halo[way, 1, :, cols])
+    def halo_chunk(side):
+        back = 1 - side
+
+        @pl.when(outer[back])
+        def _():
+            halo_copy(side, 3).wait_recv()
+            att[...] = att[...] + far_in[side].astype(F32)
+
+        @pl.when(~outer[back])
+        def _():
+            for a in range(2):
+                halo_copy(side, a).wait_recv()
+            for h in range(H):
+                cols = slice(h * DH, (h + 1) * DH)
+                weights = silu_of_half(dot_t(q_ref[:, cols], halo[side, 0, :, cols]) * maskh[2 * side])
+                att[:, cols] = att[:, cols] + dot(weights, halo[side, 1, :, cols])
+
+    def far_chunk(side):
+        back = 1 - side
+
+        @pl.when(inner[back])
+        def _():
+            halo_copy(side, 2).wait_recv()
+            for h in range(H):
+                cols = slice(h * DH, (h + 1) * DH)
+                weights = silu_of_half(dot_t(halo[side, 2, :, cols], k_ref[:, cols]) * maskh[3 + side])
+                far_out[back, :, cols] = dot(weights, v_ref[:, cols]).astype(BF16)
+            halo_copy(back, 3).start()
 
     def hist_chunk(t):
         z_ = z_of(t)
@@ -266,7 +307,6 @@
             more = dot(weights, values)
             oh[h] = more if t == 0 else oh[h] + more
 
-    halo_at = {1: [(0, 0)], 3: [(0, 1)], 5: [(1, 0)], 7: [(1, 1)]}
     for t in range(1, NZL):
         z_ = z_of(t)
         for a in range(2):
@@ -276,10 +316,15 @@
             def _():
                 hop_z(a, z_).start()
 
-        for way, a in halo_at.get(t, []):
-            halo_copy(way, a).start()
         if t == 1:
+            near_copies([0], plain)
             own_chunk()
+        if t == 2:
+            near_copies([1], wraps)
+            for side in range(2):
+                far_chunk(side)
+        if t == 3:
+            near_copies([1], plain)
         if t == 2:
             for z_ in range(NZL):
                 @pl.when((core != zh) | (z != z_))
@@ -356,8 +401,10 @@
             to_head(i, d).wait_send()
         from_head(d).wait_send()
     for way in range(2):
-        for a in range(2):
-            halo_copy(way, a).wait_send()
+        for a, sent in enumerate([~inner[way], ~inner[way], outer[way], inner[way]]):
+            @pl.when(sent)
+            def _():
+                halo_copy(way, a).wait_send()
 
     @pl.when(core == zh)
     def _():
@@ -393,13 +440,15 @@
             pltpu.VMEM((HEADS, NY * rows, DH), F32),
             pltpu.VMEM((NY, rows, SHARE), BF16),
             pltpu.VMEM((NY, rows, SHARE), BF16),
-            pltpu.VMEM((2, 2, rows, width), BF16),
+            pltpu.VMEM((2, 3, rows, width), BF16),
+            pltpu.VMEM((2, rows, width), BF16),
+            pltpu.VMEM((2, rows, width), BF16),
             pltpu.VMEM(weight.shape, BF16),
             pltpu.VMEM((NZH, NX, NY, NZL, weight.shape[0], 2 * weight.shape[1]), BF16),
-            pltpu.VMEM((3, rows, rows), F32),
+            pltpu.VMEM((5, rows, rows), F32),
             pltpu.VMEM((rows, width), F32),
             dma((11,)), dma((2, NZL)), dma((2, 2)), dma((2, NZL)), dma((3, NY - 1)), dma((3, NY - 1)),
-            dma((NY - 1,)), dma((NY - 1,)), dma((2, 2)), dma((2, 2)),
+            dma((NY - 1,)), dma((NY - 1,)), dma((2, 4)), dma((2, 4)),
             dma, dma, dma((NZH * NZL - 1,)), dma((NZL,)), dma((NY - 1,)), dma((NY - 1,)),
             dma((NX - 1,)), dma((NX - 1,)), dma((NX,)), dma((NX,)),
         ],

time: 75 us -> 77.3 us (1.031)
  Pallas kernels: 73.2 us -> 75.5 us
    pallas_call x1, Pallas kernels: 73.2 us -> 75.5 us  [shards(): pl.pallas_call(kernel, out_shape=jax.ShapeDtypeStruct((rows, width), BF16...]
where the time goes in v3:
time: 77.3 us; the launch traced here: 77.2 us
  Pallas kernels  75.5 us (98%)
  local copies, waits for them, and re-layouts  1.67 us (2%)
    pallas_call x1, Pallas kernels, shards(): pl.pallas_call(kernel, out_shape=jax.ShapeDtypeStruct((rows, width), BF16...  75.5 us
    unnamed x1, local copies, waits for them, and re-layouts  1.67 us

profile of v3, /device:TPU:6, one launch (start us, length us, event | category | flops | bytes accessed | tf_op | source)
XLA Modules:
  0.0 77.2 jit_solution(3605774541785724456)
XLA Ops:
  0.0 75.5 %shard_map.100 = bf16[128,1024]{1,0:T(8,128)(2,1)} custom-call(bf16[128,1024]{1,0:T(8,128)(2,1)} %bitcast.9, bf16[128,1024]{1,0:T(8,128)(2,1)} %bitcast.10, bf16[128,1024]{1,0:T(8,128)(2,1)} %bitcast.11, bf16[128,1024]{1,0:T(8,128)(2,1)} %bitcast.12, bf16[128,1024]{1,0:T(8,128)(2,1)} %bitcast.13, bf16[32,1024]{1,0:T(8,128)(2,1)} %bitcast.14, ...), custom_call_target="tpu_custom_call" | custom-call | tf_op jit(solution)/shard_map/pallas_call | solution.py:428
  75.5 1.7 %copy.12 = bf16[1,128,1024]{2,1,0:T(8,128)(2,1)} copy(bf16[1,128,1024]{2,1,0:T(8,128)(2,1)} %bitcast.8) | data formatting | bytes 524288

commit v4 on v3

--- a/solution.py
+++ b/solution.py
@@ -317,6 +317,21 @@
                 hop_z(a, z_).start()
 
         if t == 1:
+            for z_ in range(NZL):
+                @pl.when((core != zh) | (z != z_))
+                def _():
+                    there = wb.at[core, x, y, z_]
+                    remote(there, there, wz_send.at[0], wz_recv.at[z_], other_core).wait_recv()
+            for d in range(1, NY):
+                tile_y(d).start()
+        if t == 2:
+            for d in range(1, NY):
+                there = wb.at[core, x, lax.rem(y + NY - d, NY)]
+                remote(there, there, wy_send.at[0], wy_recv.at[d - 1], other_core).wait_recv()
+            for d in range(1, NX):
+                tile_x(d).start()
+            tile_out(0).start()
+        if t == 1:
             near_copies([0], plain)
             own_chunk()
         if t == 2:
@@ -325,22 +340,12 @@
                 far_chunk(side)
         if t == 3:
             near_copies([1], plain)
-        if t == 2:
-            for z_ in range(NZL):
-                @pl.when((core != zh) | (z != z_))
-                def _():
-                    there = wb.at[core, x, y, z_]
-                    remote(there, there, wz_send.at[0], wz_recv.at[z_], other_core).wait_recv()
-            for d in range(1, NY):
-                tile_y(d).start()
-        if t == 4:
-            for d in range(1, NY):
-                there = wb.at[core, x, lax.rem(y + NY - d, NY)]
-                remote(there, there, wy_send.at[0], wy_recv.at[d - 1], other_core).wait_recv()
+        hist_chunk(t - 1)
+        if t == 6:
             for d in range(1, NX):
-                tile_x(d).start()
-            tile_out(0).start()
-        hist_chunk(t - 1)
+                there = wb.at[core, lax.rem(x + NX - d, NX)]
+                remote(there, there, wx_send.at[0], wx_recv.at[d - 1], other_core).wait_recv()
+                tile_out(NX - d).start()
     hist_chunk(NZL - 1)
     for y_ in range(NY):
         for h in range(HEADS):
@@ -348,10 +353,6 @@
     for d in range(1, NY):
         from_head(d).start()
     part_in[y] = part_out[y]
-    for d in range(1, NX):
-        there = wb.at[core, lax.rem(x + NX - d, NX)]
-        remote(there, there, wx_send.at[0], wx_recv.at[d - 1], other_core).wait_recv()
-        tile_out(NX - d).start()
     halo_chunk(0)
     halo_chunk(1)
 

time: 77.3 us -> 81.8 us (1.058)
  Pallas kernels: 75.5 us -> 79.9 us
    pallas_call x1, Pallas kernels: 75.5 us -> 79.9 us  [shards(): pl.pallas_call(kernel, out_shape=jax.ShapeDtypeStruct((rows, width), BF16...]
where the time goes in v4:
time: 81.8 us; the launch traced here: 81.6 us
  Pallas kernels  79.9 us (98%)
  local copies, waits for them, and re-layouts  1.67 us (2%)
    pallas_call x1, Pallas kernels, shards(): pl.pallas_call(kernel, out_shape=jax.ShapeDtypeStruct((rows, width), BF16...  79.9 us
    unnamed x1, local copies, waits for them, and re-layouts  1.67 us

profile of v4, /device:TPU:6, one launch (start us, length us, event | category | flops | bytes accessed | tf_op | source)
XLA Modules:
  0.0 81.6 jit_solution(10804737754635839420)
XLA Ops:
  0.0 79.9 %shard_map.100 = bf16[128,1024]{1,0:T(8,128)(2,1)} custom-call(bf16[128,1024]{1,0:T(8,128)(2,1)} %bitcast.9, bf16[128,1024]{1,0:T(8,128)(2,1)} %bitcast.10, bf16[128,1024]{1,0:T(8,128)(2,1)} %bitcast.11, bf16[128,1024]{1,0:T(8,128)(2,1)} %bitcast.12, bf16[128,1024]{1,0:T(8,128)(2,1)} %bitcast.13, bf16[32,1024]{1,0:T(8,128)(2,1)} %bitcast.14, ...), custom_call_target="tpu_custom_call" | custom-call | tf_op jit(solution)/shard_map/pallas_call | solution.py:429
  79.9 1.7 %copy.12 = bf16[1,128,1024]{2,1,0:T(8,128)(2,1)} copy(bf16[1,128,1024]{2,1,0:T(8,128)(2,1)} %bitcast.8) | data formatting | bytes 524288

commit v5 on v3

--- a/solution.py
+++ b/solution.py
@@ -181,12 +181,10 @@
         here = wb.at[core, lax.rem(x + d, NX)]
         return remote(here, here, wo_send.at[d], wo_recv.at[d], other_core)
 
+    tile_core.start()
     for i in range(3):
         for d in range(1, NY):
             to_head(i, d).start()
-    near_copies([0], wraps)
-    near_copies([2], outer)
-    tile_core.start()
 
     for copy in incoming[:3]:
         copy.wait()
@@ -228,6 +226,18 @@
             seen = seen & (tall[r + 1] == wide[b + 1])
             maskh[i] = jnp.where(seen, half_factor, 0.0)
 
+    tile_core.wait()
+    mine, theirs = w_ref[...].astype(F32), wtmp[...].astype(F32)
+    tile = jnp.where(
+        core == 0, jnp.concatenate([mine, theirs], axis=1), jnp.concatenate([theirs, mine], axis=1)
+    ).astype(BF16)
+
+    @pl.when(core == zh)
+    def _():
+        wb[core, x, y, z] = tile
+        for d in range(1, NZH * NZL):
+            tile_z(d).start()
+
     for copy in incoming[3:5]:
         copy.wait()
     for a in range(2):
@@ -242,18 +252,8 @@
         def _():
             own_z(a, 1).start()
 
-    tile_core.wait()
-    mine, theirs = w_ref[...].astype(F32), wtmp[...].astype(F32)
-    tile = jnp.where(
-        core == 0, jnp.concatenate([mine, theirs], axis=1), jnp.concatenate([theirs, mine], axis=1)
-    ).astype(BF16)
-
-    @pl.when(core == zh)
-    def _():
-        wb[core, x, y, z] = tile
-        for d in range(1, NZH * NZL):
-            tile_z(d).start()
-
+    near_copies([0], wraps)
+    near_copies([2], outer)
     make_mask()
 
     def own_chunk():
@@ -321,10 +321,11 @@
             own_chunk()
         if t == 2:
             near_copies([1], wraps)
+        if t == 3:
+            near_copies([1], plain)
+        if t == 4:
             for side in range(2):
                 far_chunk(side)
-        if t == 3:
-            near_copies([1], plain)
         if t == 2:
             for z_ in range(NZL):
                 @pl.when((core != zh) | (z != z_))
@@ -333,7 +334,7 @@
                     remote(there, there, wz_send.at[0], wz_recv.at[z_], other_core).wait_recv()
             for d in range(1, NY):
                 tile_y(d).start()
-        if t == 4:
+        if t == 3:
             for d in range(1, NY):
                 there = wb.at[core, x, lax.rem(y + NY - d, NY)]
                 remote(there, there, wy_send.at[0], wy_recv.at[d - 1], other_core).wait_recv()

time: 77.3 us -> 77.5 us (level)
  no operation moved by 1% of the time
where the time goes in v5:
time: 77.5 us; the launch traced here: 77.4 us
  Pallas kernels  75.7 us (98%)
  local copies, waits for them, and re-layouts  1.67 us (2%)
    pallas_call x1, Pallas kernels, shards(): pl.pallas_call(kernel, out_shape=jax.ShapeDtypeStruct((rows, width), BF16...  75.7 us
    unnamed x1, local copies, waits for them, and re-layouts  1.67 us

profile of v5, /device:TPU:6, one launch (start us, length us, event | category | flops | bytes accessed | tf_op | source)
XLA Modules:
  0.0 77.4 jit_solution(15058213528908762290)
XLA Ops:
  0.0 75.7 %shard_map.100 = bf16[128,1024]{1,0:T(8,128)(2,1)} custom-call(bf16[128,1024]{1,0:T(8,128)(2,1)} %bitcast.9, bf16[128,1024]{1,0:T(8,128)(2,1)} %bitcast.10, bf16[128,1024]{1,0:T(8,128)(2,1)} %bitcast.11, bf16[128,1024]{1,0:T(8,128)(2,1)} %bitcast.12, bf16[128,1024]{1,0:T(8,128)(2,1)} %bitcast.13, bf16[32,1024]{1,0:T(8,128)(2,1)} %bitcast.14, ...), custom_call_target="tpu_custom_call" | custom-call | tf_op jit(solution)/shard_map/pallas_call | solution.py:429
  75.7 1.7 %copy.12 = bf16[1,128,1024]{2,1,0:T(8,128)(2,1)} copy(bf16[1,128,1024]{2,1,0:T(8,128)(2,1)} %bitcast.8) | data formatting | bytes 524288

commit v6 on v2

--- a/solution.py
+++ b/solution.py
@@ -237,13 +237,13 @@
 
     make_mask()
 
-    def own_chunk():
-        for copy in incoming[6:9]:
-            copy.wait()
-        for h in range(H):
-            cols = slice(h * DH, (h + 1) * DH)
-            weights = silu_of_half(dot_t(q_ref[:, cols], k_ref[:, cols]) * maskh[1])
-            att[:, cols] = dot(weights, v_ref[:, cols])
+    def own_head(h):
+        if h == 0:
+            for copy in incoming[6:9]:
+                copy.wait()
+        cols = slice(h * DH, (h + 1) * DH)
+        weights = silu_of_half(dot_t(q_ref[:, cols], k_ref[:, cols]) * maskh[1])
+        att[:, cols] = dot(weights, v_ref[:, cols])
 
     def halo_chunk(way):
         for a in range(2):
@@ -253,19 +253,18 @@
             weights = silu_of_half(dot_t(q_ref[:, cols], halo[way, 0, :, cols]) * maskh[2 * way])
             att[:, cols] = att[:, cols] + dot(weights, halo[way, 1, :, cols])
 
-    def hist_chunk(t):
+    def hist_head(t, h):
         z_ = z_of(t)
-        if t == 0:
+        if t == 0 and h == 0:
             incoming[5].wait()
             for d in range(1, NY):
                 at_head(2, d)
-        for h in range(HEADS):
-            cols = slice(h * DH, (h + 1) * DH)
-            keys = kvh[z_, 0, :, :, cols].reshape(-1, DH)
-            values = kvh[z_, 1, :, :, cols].reshape(-1, DH)
-            weights = silu_of_half(dot_t(qh[:, :, cols].reshape(-1, DH), keys) * half_factor)
-            more = dot(weights, values)
-            oh[h] = more if t == 0 else oh[h] + more
+        cols = slice(h * DH, (h + 1) * DH)
+        keys = kvh[z_, 0, :, :, cols].reshape(-1, DH)
+        values = kvh[z_, 1, :, :, cols].reshape(-1, DH)
+        weights = silu_of_half(dot_t(qh[:, :, cols].reshape(-1, DH), keys) * half_factor)
+        more = dot(weights, values)
+        oh[h] = more if t == 0 else oh[h] + more
 
     halo_at = {1: [(1, 0)], 3: [(0, 1)], 5: [(1, 1)]}
     for t in range(1, NZL):
@@ -277,10 +276,12 @@
             def _():
                 hop_z(a, z_).start()
 
+            if a == 0:
+                hist_head(t - 1, 0)
+                if t < 5:
+                    own_head(2 * t - 2)
         for way, a in halo_at.get(t, []):
             halo_copy(way, a).start()
-        if t == 1:
-            own_chunk()
         if t == 2:
             for z_ in range(NZL):
                 @pl.when((core != zh) | (z != z_))
@@ -296,8 +297,11 @@
             for d in range(1, NX):
                 tile_x(d).start()
             tile_out(0).start()
-        hist_chunk(t - 1)
-    hist_chunk(NZL - 1)
+        hist_head(t - 1, 1)
+        if t < 5:
+            own_head(2 * t - 1)
+    for h in range(HEADS):
+        hist_head(NZL - 1, h)
     for y_ in range(NY):
         for h in range(HEADS):
             part_out[y_, :, h * DH:(h + 1) * DH] = oh[h, y_ * rows:(y_ + 1) * rows].astype(BF16)

time: 76.9 us -> 76.8 us (level)
  no operation moved by 1% of the time
where the time goes in v6:
time: 76.8 us; the launch traced here: 76.7 us
  Pallas kernels  75 us (98%)
  local copies, waits for them, and re-layouts  1.67 us (2%)
    pallas_call x1, Pallas kernels, shards(): pl.pallas_call(kernel, out_shape=jax.ShapeDtypeStruct((rows, width), BF16...  75 us
    unnamed x1, local copies, waits for them, and re-layouts  1.67 us

profile of v6, /device:TPU:6, one launch (start us, length us, event | category | flops | bytes accessed | tf_op | source)
XLA Modules:
  0.0 76.7 jit_solution(6588047347649522798)
XLA Ops:
  0.0 75.0 %shard_map.100 = bf16[128,1024]{1,0:T(8,128)(2,1)} custom-call(bf16[128,1024]{1,0:T(8,128)(2,1)} %bitcast.9, bf16[128,1024]{1,0:T(8,128)(2,1)} %bitcast.10, bf16[128,1024]{1,0:T(8,128)(2,1)} %bitcast.11, bf16[128,1024]{1,0:T(8,128)(2,1)} %bitcast.12, bf16[128,1024]{1,0:T(8,128)(2,1)} %bitcast.13, bf16[32,1024]{1,0:T(8,128)(2,1)} %bitcast.14, ...), custom_call_target="tpu_custom_call" | custom-call | tf_op jit(solution)/shard_map/pallas_call | solution.py:386
  75.0 1.7 %copy.12 = bf16[1,128,1024]{2,1,0:T(8,128)(2,1)} copy(bf16[1,128,1024]{2,1,0:T(8,128)(2,1)} %bitcast.8) | data formatting | bytes 524288

commit v7 on v6

--- a/solution.py
+++ b/solution.py
@@ -107,7 +107,8 @@
 
     def z_of(t):
         both = 2 * jnp.minimum(z, NZL - 1 - z)
-        turn = z - (t + 1) // 2 if t % 2 else z + t // 2
+        side = jnp.where(2 * z < NZL, -1, 1)
+        turn = z + side * ((t + 1) // 2 if t % 2 else -(t // 2))
         return jnp.where(t <= both, turn, jnp.where(2 * z < NZL, t, NZL - 1 - t))
 
     def to_head(i, d):
@@ -150,6 +151,15 @@
             on_cand(nxt if way == 0 else prv),
         )
 
+    wraps = (z == NZL - 1, z == 0)
+    beside = (~wraps[0], ~wraps[1])
+
+    def near_copies(a, when):
+        for way in range(2):
+            @pl.when(when[way])
+            def _():
+                halo_copy(way, a).start()
+
     tile_core = remote(w_hbm, wtmp, wc_send, wc_recv, other_core)
 
     def tile_z(d):
@@ -172,7 +182,7 @@
     for i in range(3):
         for d in range(1, NY):
             to_head(i, d).start()
-    halo_copy(0, 0).start()
+    near_copies(0, beside)
     tile_core.start()
 
     for copy in incoming[:3]:
@@ -266,7 +276,7 @@
         more = dot(weights, values)
         oh[h] = more if t == 0 else oh[h] + more
 
-    halo_at = {1: [(1, 0)], 3: [(0, 1)], 5: [(1, 1)]}
+    near_at = {1: (0, wraps), 3: (1, beside), 5: (1, wraps)}
     for t in range(1, NZL):
         z_ = z_of(t)
         for a in range(2):
@@ -280,8 +290,8 @@
                 hist_head(t - 1, 0)
                 if t < 5:
                     own_head(2 * t - 2)
-        for way, a in halo_at.get(t, []):
-            halo_copy(way, a).start()
+        if t in near_at:
+            near_copies(*near_at[t])
         if t == 2:
             for z_ in range(NZL):
                 @pl.when((core != zh) | (z != z_))

time: 76.8 us -> 74.9 us (0.975)
  Pallas kernels: 75 us -> 73.1 us
    pallas_call x1, Pallas kernels: 75 us -> 73.1 us  [shards(): pl.pallas_call(kernel, out_shape=jax.ShapeDtypeStruct((rows, width), BF16...]
where the time goes in v7:
time: 74.9 us; the launch traced here: 74.8 us
  Pallas kernels  73.1 us (98%)
  local copies, waits for them, and re-layouts  1.67 us (2%)
    pallas_call x1, Pallas kernels, shards(): pl.pallas_call(kernel, out_shape=jax.ShapeDtypeStruct((rows, width), BF16...  73.1 us
    unnamed x1, local copies, waits for them, and re-layouts  1.67 us

profile of v7, /device:TPU:6, one launch (start us, length us, event | category | flops | bytes accessed | tf_op | source)
XLA Modules:
  0.0 74.8 jit_solution(16291734471063834657)
XLA Ops:
  0.0 73.1 %shard_map.100 = bf16[128,1024]{1,0:T(8,128)(2,1)} custom-call(bf16[128,1024]{1,0:T(8,128)(2,1)} %bitcast.9, bf16[128,1024]{1,0:T(8,128)(2,1)} %bitcast.10, bf16[128,1024]{1,0:T(8,128)(2,1)} %bitcast.11, bf16[128,1024]{1,0:T(8,128)(2,1)} %bitcast.12, bf16[128,1024]{1,0:T(8,128)(2,1)} %bitcast.13, bf16[32,1024]{1,0:T(8,128)(2,1)} %bitcast.14, ...), custom_call_target="tpu_custom_call" | custom-call | tf_op jit(solution)/shard_map/pallas_call | solution.py:396
  73.1 1.7 %copy.12 = bf16[1,128,1024]{2,1,0:T(8,128)(2,1)} copy(bf16[1,128,1024]{2,1,0:T(8,128)(2,1)} %bitcast.8) | data formatting | bytes 524288

commit v8 on v7

--- a/solution.py
+++ b/solution.py
@@ -255,13 +255,14 @@
         weights = silu_of_half(dot_t(q_ref[:, cols], k_ref[:, cols]) * maskh[1])
         att[:, cols] = dot(weights, v_ref[:, cols])
 
-    def halo_chunk(way):
+    def halo_chunk(side):
         for a in range(2):
-            halo_copy(way, a).wait_recv()
+            here = halo.at[side, a]
+            remote(here, here, halo_send.at[0, 0], halo_recv.at[side, a], other_core).wait_recv()
         for h in range(H):
             cols = slice(h * DH, (h + 1) * DH)
-            weights = silu_of_half(dot_t(q_ref[:, cols], halo[way, 0, :, cols]) * maskh[2 * way])
-            att[:, cols] = att[:, cols] + dot(weights, halo[way, 1, :, cols])
+            weights = silu_of_half(dot_t(q_ref[:, cols], halo[side, 0, :, cols]) * maskh[2 * side])
+            att[:, cols] = att[:, cols] + dot(weights, halo[side, 1, :, cols])
 
     def hist_head(t, h):
         z_ = z_of(t)
@@ -276,7 +277,7 @@
         more = dot(weights, values)
         oh[h] = more if t == 0 else oh[h] + more
 
-    near_at = {1: (0, wraps), 3: (1, beside), 5: (1, wraps)}
+    near_at = {1: (0, wraps), 3: (1, beside), 4: (1, wraps)}
     for t in range(1, NZL):
         z_ = z_of(t)
         for a in range(2):
@@ -322,8 +323,9 @@
         there = wb.at[core, lax.rem(x + NX - d, NX)]
         remote(there, there, wx_send.at[0], wx_recv.at[d - 1], other_core).wait_recv()
         tile_out(NX - d).start()
-    halo_chunk(0)
-    halo_chunk(1)
+    near = jnp.where(z == 0, 1, 0)
+    halo_chunk(near)
+    halo_chunk(1 - near)
 
     for copy in incoming[9:]:
         copy.wait()

time: 74.9 us -> 73.3 us (0.979)
  Pallas kernels: 73.1 us -> 70.8 us
    pallas_call x1, Pallas kernels: 73.1 us -> 70.8 us  [shards(): pl.pallas_call(kernel, out_shape=jax.ShapeDtypeStruct((rows, width), BF16...]
where the time goes in v8:
time: 73.3 us; the launch traced here: 72.5 us
  Pallas kernels  70.8 us (97%)
  local copies, waits for them, and re-layouts  1.67 us (2%)
    pallas_call x1, Pallas kernels, shards(): pl.pallas_call(kernel, out_shape=jax.ShapeDtypeStruct((rows, width), BF16...  70.8 us
    unnamed x1, local copies, waits for them, and re-layouts  1.67 us

profile of v8, /device:TPU:6, one launch (start us, length us, event | category | flops | bytes accessed | tf_op | source)
XLA Modules:
  0.0 72.5 jit_solution(759099439475552005)
XLA Ops:
  0.0 70.8 %shard_map.100 = bf16[128,1024]{1,0:T(8,128)(2,1)} custom-call(bf16[128,1024]{1,0:T(8,128)(2,1)} %bitcast.9, bf16[128,1024]{1,0:T(8,128)(2,1)} %bitcast.10, bf16[128,1024]{1,0:T(8,128)(2,1)} %bitcast.11, bf16[128,1024]{1,0:T(8,128)(2,1)} %bitcast.12, bf16[128,1024]{1,0:T(8,128)(2,1)} %bitcast.13, bf16[32,1024]{1,0:T(8,128)(2,1)} %bitcast.14, ...), custom_call_target="tpu_custom_call" | custom-call | tf_op jit(solution)/shard_map/pallas_call | solution.py:398
  70.8 1.7 %copy.12 = bf16[1,128,1024]{2,1,0:T(8,128)(2,1)} copy(bf16[1,128,1024]{2,1,0:T(8,128)(2,1)} %bitcast.8) | data formatting | bytes 524288

commit v9 on v8

--- a/solution.py
+++ b/solution.py
@@ -301,7 +301,7 @@
                     remote(there, there, wz_send.at[0], wz_recv.at[z_], other_core).wait_recv()
             for d in range(1, NY):
                 tile_y(d).start()
-        if t == 4:
+        if t == 3:
             for d in range(1, NY):
                 there = wb.at[core, x, lax.rem(y + NY - d, NY)]
                 remote(there, there, wy_send.at[0], wy_recv.at[d - 1], other_core).wait_recv()

time: 73.3 us -> 73.3 us (level)
  no operation moved by 1% of the time
where the time goes in v9:
time: 73.3 us; the launch traced here: 72.2 us
  Pallas kernels  70.5 us (96%)
  local copies, waits for them, and re-layouts  1.67 us (2%)
    pallas_call x1, Pallas kernels, shards(): pl.pallas_call(kernel, out_shape=jax.ShapeDtypeStruct((rows, width), BF16...  70.5 us
    unnamed x1, local copies, waits for them, and re-layouts  1.67 us

profile of v9, /device:TPU:6, one launch (start us, length us, event | category | flops | bytes accessed | tf_op | source)
XLA Modules:
  0.0 72.2 jit_solution(6886906002951077820)
XLA Ops:
  0.0 70.5 %shard_map.100 = bf16[128,1024]{1,0:T(8,128)(2,1)} custom-call(bf16[128,1024]{1,0:T(8,128)(2,1)} %bitcast.9, bf16[128,1024]{1,0:T(8,128)(2,1)} %bitcast.10, bf16[128,1024]{1,0:T(8,128)(2,1)} %bitcast.11, bf16[128,1024]{1,0:T(8,128)(2,1)} %bitcast.12, bf16[128,1024]{1,0:T(8,128)(2,1)} %bitcast.13, bf16[32,1024]{1,0:T(8,128)(2,1)} %bitcast.14, ...), custom_call_target="tpu_custom_call" | custom-call | tf_op jit(solution)/shard_map/pallas_call | solution.py:398
  70.5 1.7 %copy.12 = bf16[1,128,1024]{2,1,0:T(8,128)(2,1)} copy(bf16[1,128,1024]{2,1,0:T(8,128)(2,1)} %bitcast.8) | data formatting | bytes 524288

commit v10 on v9

--- a/solution.py
+++ b/solution.py
@@ -277,7 +277,7 @@
         more = dot(weights, values)
         oh[h] = more if t == 0 else oh[h] + more
 
-    near_at = {1: (0, wraps), 3: (1, beside), 4: (1, wraps)}
+    near_at = {1: (0, wraps), 3: (1, wraps), 4: (1, beside)}
     for t in range(1, NZL):
         z_ = z_of(t)
         for a in range(2):

time: 73.3 us -> 74.5 us (1.016); the launches traced: 72.2 us -> 74.4 us
  Pallas kernels: 70.5 us -> 72.7 us
    pallas_call x1, Pallas kernels: 70.5 us -> 72.7 us  [shards(): pl.pallas_call(kernel, out_shape=jax.ShapeDtypeStruct((rows, width), BF16...]
where the time goes in v10:
time: 74.5 us; the launch traced here: 74.4 us
  Pallas kernels  72.7 us (98%)
  local copies, waits for them, and re-layouts  1.67 us (2%)
    pallas_call x1, Pallas kernels, shards(): pl.pallas_call(kernel, out_shape=jax.ShapeDtypeStruct((rows, width), BF16...  72.7 us
    unnamed x1, local copies, waits for them, and re-layouts  1.67 us

profile of v10, /device:TPU:6, one launch (start us, length us, event | category | flops | bytes accessed | tf_op | source)
XLA Modules:
  0.0 74.4 jit_solution(11231773660095749177)
XLA Ops:
  0.0 72.7 %shard_map.100 = bf16[128,1024]{1,0:T(8,128)(2,1)} custom-call(bf16[128,1024]{1,0:T(8,128)(2,1)} %bitcast.9, bf16[128,1024]{1,0:T(8,128)(2,1)} %bitcast.10, bf16[128,1024]{1,0:T(8,128)(2,1)} %bitcast.11, bf16[128,1024]{1,0:T(8,128)(2,1)} %bitcast.12, bf16[128,1024]{1,0:T(8,128)(2,1)} %bitcast.13, bf16[32,1024]{1,0:T(8,128)(2,1)} %bitcast.14, ...), custom_call_target="tpu_custom_call" | custom-call | tf_op jit(solution)/shard_map/pallas_call | solution.py:398
  72.7 1.7 %copy.12 = bf16[1,128,1024]{2,1,0:T(8,128)(2,1)} copy(bf16[1,128,1024]{2,1,0:T(8,128)(2,1)} %bitcast.8) | data formatting | bytes 524288

commit v11 on v9

--- a/solution.py
+++ b/solution.py
@@ -30,11 +30,11 @@
 
 def kernel(
     q_hbm, k_hbm, v_hbm, gate_hbm, res_hbm, hk_hbm, hv_hbm, ids_hbm, pat_hbm, w_hbm,
-    out_ref,
-    rows5, ids_ref, pat_ref, w_ref,
+    out_hbm,
+    out_buf, rows5, ids_ref, pat_ref, w_ref,
     kvh, qh, oh, part_out, part_in, halo, wtmp, wb, maskh, att,
     in_sem, kv_recv, own_send, z_send, ys_send, ys_recv, o_send, o_recv, halo_send, halo_recv,
-    wc_send, wc_recv, wz_send, wz_recv, wy_send, wy_recv, wx_send, wx_recv, wo_send, wo_recv,
+    wc_send, wc_recv, wz_send, wz_recv, wy_send, wy_recv, wx_send, wx_recv, wo_send, wo_recv, out_sem,
 ):
     u, c = lax.axis_index("users"), lax.axis_index("cand")
     core = lax.rem(u, NCORE)
@@ -44,6 +44,10 @@
     y = c // NZL
     rows = q_hbm.shape[0]
     q_ref, k_ref, v_ref, gate_ref, res_ref = [rows5.at[i] for i in range(5)]
+
+    def leaving(x_):
+        cols = slice(x_ * 2 * DH, (x_ + 1) * 2 * DH)
+        return pltpu.make_async_copy(out_buf.at[:, cols], out_hbm.at[:, cols], out_sem.at[x_])
 
     def share(y_):
         return pl.ds(pl.multiple_of(y_ * SHARE, SHARE), SHARE)
@@ -311,6 +315,10 @@
         hist_head(t - 1, 1)
         if t < 5:
             own_head(2 * t - 1)
+    for d in range(1, NX):
+        there = wb.at[core, lax.rem(x + NX - d, NX)]
+        remote(there, there, wx_send.at[0], wx_recv.at[d - 1], other_core).wait_recv()
+        tile_out(NX - d).start()
     for h in range(HEADS):
         hist_head(NZL - 1, h)
     for y_ in range(NY):
@@ -319,10 +327,6 @@
     for d in range(1, NY):
         from_head(d).start()
     part_in[y] = part_out[y]
-    for d in range(1, NX):
-        there = wb.at[core, lax.rem(x + NX - d, NX)]
-        remote(there, there, wx_send.at[0], wx_recv.at[d - 1], other_core).wait_recv()
-        tile_out(NX - d).start()
     near = jnp.where(z == 0, 1, 0)
     halo_chunk(near)
     halo_chunk(1 - near)
@@ -348,7 +352,8 @@
         weight = jnp.concatenate(
             [wb[0, x_].reshape(-1, DH), wb[1, x_].reshape(-1, DH)], axis=1
         )
-        out_ref[:, cols] = (res_ref[:, cols].astype(F32) + dot(gated, weight)).astype(BF16)
+        out_buf[:, cols] = (res_ref[:, cols].astype(F32) + dot(gated, weight)).astype(BF16)
+        leaving(x_).start()
 
     @pl.when(z < NZL - 1)
     def _():
@@ -387,20 +392,21 @@
         tile_x(d).wait_send()
     for d in range(NX):
         tile_out(d).wait_send()
+        leaving(d).wait()
 
 
 def shards(q, k, v, gate, resid, hk, hv, ids, pattern, weight):
     rows, width = q.shape[1:]
     hist = hk.shape[1]
     hbm = pl.BlockSpec(memory_space=pl.ANY)
-    vmem = pl.BlockSpec(memory_space=pltpu.VMEM)
     dma = pltpu.SemaphoreType.DMA
     out = pl.pallas_call(
         kernel,
         out_shape=jax.ShapeDtypeStruct((rows, width), BF16),
         in_specs=[hbm] * 10,
-        out_specs=vmem,
+        out_specs=hbm,
         scratch_shapes=[
+            pltpu.VMEM((rows, width), BF16),
             pltpu.VMEM((5, rows, width), BF16),
             pltpu.VMEM(ids.shape, ids.dtype),
             pltpu.VMEM(pattern.shape, pattern.dtype),
@@ -418,7 +424,7 @@
             dma((11,)), dma((2, NZL)), dma((2, 2)), dma((2, NZL)), dma((3, NY - 1)), dma((3, NY - 1)),
             dma((NY - 1,)), dma((NY - 1,)), dma((2, 2)), dma((2, 2)),
             dma, dma, dma((NZH * NZL - 1,)), dma((NZL,)), dma((NY - 1,)), dma((NY - 1,)),
-            dma((NX - 1,)), dma((NX - 1,)), dma((NX,)), dma((NX,)),
+            dma((NX - 1,)), dma((NX - 1,)), dma((NX,)), dma((NX,)), dma((NX,)),
         ],
         compiler_params=pltpu.CompilerParams(
             collective_id=0, has_side_effects=True, vmem_limit_bytes=60 * 1024 * 1024

time: 73.3 us -> 73.3 us (level)
  no operation moved by 1% of the time
where the time goes in v11:
time: 73.3 us; the launch traced here: 72.2 us
  Pallas kernels  70.5 us (96%)
  local copies, waits for them, and re-layouts  1.67 us (2%)
    pallas_call x1, Pallas kernels, shards(): pl.pallas_call(kernel, out_shape=jax.ShapeDtypeStruct((rows, width), BF16...  70.5 us
    unnamed x1, local copies, waits for them, and re-layouts  1.67 us

profile of v11, /device:TPU:6, one launch (start us, length us, event | category | flops | bytes accessed | tf_op | source)
XLA Modules:
  0.0 72.2 jit_solution(1061616030636291382)
XLA Ops:
  0.0 70.5 %shard_map.100 = bf16[128,1024]{1,0:T(8,128)(2,1)} custom-call(bf16[128,1024]{1,0:T(8,128)(2,1)} %bitcast.9, bf16[128,1024]{1,0:T(8,128)(2,1)} %bitcast.10, bf16[128,1024]{1,0:T(8,128)(2,1)} %bitcast.11, bf16[128,1024]{1,0:T(8,128)(2,1)} %bitcast.12, bf16[128,1024]{1,0:T(8,128)(2,1)} %bitcast.13, bf16[32,1024]{1,0:T(8,128)(2,1)} %bitcast.14, ...), custom_call_target="tpu_custom_call" | custom-call | tf_op jit(solution)/shard_map/pallas_call | solution.py:403
  70.5 1.7 %copy.12 = bf16[1,128,1024]{2,1,0:T(8,128)(2,1)} copy(bf16[1,128,1024]{2,1,0:T(8,128)(2,1)} %bitcast.8) | data formatting | bytes 524288
